TPU v7x, 32 devices: a whole 2x2x4 slice. The times are simulated.
32 devices in a mesh: tp: 8 (over z, x), hb: 4 (over y, core).
Axes of the slice: x: 2, y: 2, z: 4, core: 2. Of those that a mesh axis runs over, the one named last changes fastest.
Arguments:
- normed: bfloat16 [512, 16384], P('hb', 'tp'), may hold values from -6 to 6
- hidden: bfloat16 [512, 26624], P('hb', 'tp'), may hold values from -6 to 6
Outputs:
- h_in: float32 [16384, 16384], P('tp', 'hb')
- h_down: float32 [26624, 3328], P(('tp', 'hb'))
All inputs are finite; a program needn't handle non-finite values.
Results may differ from a plain program's by a relative error of at most 0.0003.
Values may be sent and summed in bfloat16 or wider, within the bound.
A program may use at most 192 MiB of HBM per device.

v0:
```python
import jax
import jax.numpy as jnp
from jax import lax
from jax.sharding import PartitionSpec as P


def gram_product(left, right):
    return lax.dot_general(
        left, right, (((0,), (0,)), ((), ())), preferred_element_type=jnp.float32
    )


def per_device(normed, hidden):
    groups = lax.axis_size("hb")
    scale = 2.0 / (normed.shape[0] * groups)
    whole_rows = lax.all_gather(normed, "tp", axis=1, tiled=True)
    columns = lax.all_to_all(whole_rows, "hb", split_axis=1, concat_axis=0, tiled=True)
    part = columns
    h_in = gram_product(lax.all_gather(normed, "hb", axis=0, tiled=True), part) * scale
    part = hidden
    h_down = (
        lax.psum_scatter(gram_product(part, hidden), "hb", scatter_dimension=0, tiled=True) * scale
    )
    return (h_in, h_down)


def solution(mesh):
    return jax.shard_map(
        per_device,
        mesh=mesh,
        in_specs=(P("hb", "tp"), P("hb", "tp")),
        out_specs=(P("tp", "hb"), P(("tp", "hb"), None)),
        check_vma=False,
    )
```

profile of v0, /device:TPU:24, one launch (start us, length us, event | category | flops | bytes accessed | tf_op | source)
XLA Modules:
  0.0 441.3 jit_solution(4497799613486758380)
XLA Ops:
  7.2 0.0 copy-start
  7.2 0.0 all-gather.5.cloned.1.call-start
  7.2 2.1 copy.4
  9.3 0.0 all-gather.5.cloned.1.call-update
  9.4 0.0 all-gather.3.cloned.1.call-start
  9.4 0.7 all-gather.3.cloned.1.call-update
  10.1 0.0 reduce-scatter.2.cloned.1.call-start
  10.2 0.0 copy-done
  10.2 17.8 %fusion = f32[3328,3328]{1,0:T(8,128)} fusion(bf16[128,3328]{1,0:T(8,128)(2,1)S(1)} %copy-done), kind=kOutput, calls=%fused_computation.2 | convolution fusion | flops 2835349504 | bytes 45154304 | tf_op jit(solution)/shard_map/dot_general | solution.py:8
  27.9 0.0 reduce-scatter.2.cloned.1.call-update
  27.9 55.4 %all-gather.5.cloned.1.call-done = bf16[128,16384]{0,1:T(8,128)(2,1)} async-done(((bf16[128,2048]{0,1:T(8,128)(2,1)}), bf16[128,16384]{0,1:T(8,128)(2,1)}) %all-gather.5.cloned.1.call-update) | async-done | bytes 4194320 | tf_op jit(solution)/shard_map/all_gather | solution.py:16
  83.4 65.1 %all_to_all.19 = bf16[128,4,4096]{0,2,1:T(8,128)(2,1)} all-to-all(bf16[128,4,4096]{0,2,1:T(8,128)(2,1)} %bitcast.8), channel_id=1, replica_groups=mesh['tp'=8,'hb'=4] {'hb'}, dimensions={1} | all-to-all | bytes 8388608 | tf_op jit(solution)/shard_map/all_to_all | solution.py:17
  148.4 7.0 %copy.5 = bf16[4,128,4096]{2,1,0:T(8,128)(2,1)} copy(bf16[4,128,4096]{1,2,0:T(8,128)(2,1)} %bitcast.7) | data formatting | bytes 8388608 | tf_op jit(solution)/shard_map/all_to_all | solution.py:17
  155.4 0.0 all-gather.3.cloned.1.call-done
  155.4 0.0 copy-start.1
  155.4 24.4 %convolution_multiply_fusion = f32[2048,4096]{1,0:T(8,128)} fusion(bf16[512,2048]{1,0:T(8,128)(2,1)} %all-gather.3.cloned.1.call-done, bf16[512,4096]{1,0:T(8,128)(2,1)} %bitcast.9), kind=kOutput, calls=%fused_computation | convolution fusion | flops 8598323200 | bytes 39845888 | tf_op jit(solution)/shard_map/dot_general | solution.py:8
  179.8 245.8 %reduce-scatter.2.cloned.1.call-done = f32[832,3328]{1,0:T(8,128)} async-done(((f32[3328,3328]{1,0:T(8,128)}), f32[832,3328]{1,0:T(8,128)}) %reduce-scatter.2.cloned.1.call-update) | async-done | bytes 11075600 | tf_op jit(solution)/shard_map/reduce_scatter | solution.py:22
  425.6 9.1 %broadcast_multiply_fusion = f32[832,3328]{1,0:T(8,128)} fusion(f32[832,3328]{1,0:T(8,128)} %reduce-scatter.2.cloned.1.call-done), kind=kLoop, calls=%fused_computation.1 | loop fusion | flops 2768896 | bytes 22151168 | tf_op jit(solution)/shard_map/mul | solution.py:22
  434.8 0.0 copy-done.1
Async XLA Ops:
  7.2 3.0 copy-start
  7.2 76.2 %all-gather.5.cloned.1.call-start = ((), (), s32[]{:S(2)}) async-start(), calls=%async_computation.3 | async-start | bytes 4718592 | tf_op jit(solution)/shard_map/all_gather | solution.py:16
  9.4 146.0 %all-gather.3.cloned.1.call-start = ((), (), s32[]{:S(2)}) async-start(), calls=%async_computation.2 | async-start | bytes 2621440 | tf_op jit(solution)/shard_map/all_gather | solution.py:19
  10.1 415.5 %reduce-scatter.2.cloned.1.call-start = ((), (), s32[]{:S(2)}) async-start(), calls=%async_computation.4 | async-start | bytes 55377920 | tf_op jit(solution)/shard_map/reduce_scatter | solution.py:22
  155.4 279.4 %copy-start.1 = (bf16[128,3328]{1,0:T(8,128)(2,1)S(1)}, bf16[128,3328]{1,0:T(8,128)(2,1)}, u32[]{:S(2)}) copy-start(bf16[128,3328]{1,0:T(8,128)(2,1)} %param.3) | copy-start | bytes 2555908
Sparse Core Ops, SparseCore 0:
  10.7 72.5 all-gather.4
  84.9 33.9 all-gather.2
  121.5 304.0 reduce-scatter.1
where the time goes:
time: 443 us; the launch traced here: 441 us
  waiting for transfers between devices  302 us (68%)
  blocking collectives  65.1 us (15%)
  matrix products  42.2 us (10%)
  between operations  13.8 us (3%)
  other arithmetic  9.14 us (2%)
  local copies, waits for them, and re-layouts  9.07 us (2%)
    reduce_scatter x1, waiting for transfers between devices, per_device(): lax.psum_scatter(gram_product(part, hidden), 'hb', scatter_dimension=0, t...  246 us
    all_to_all x1, blocking collectives, per_device(): lax.all_to_all(whole_rows, 'hb', split_axis=1, concat_axis=0, tiled=True)  65.1 us
    all_gather x1, waiting for transfers between devices, per_device(): whole_rows = lax.all_gather(normed, 'tp', axis=1, tiled=True)  55.4 us
    dot_general x2, matrix products, gram_product(): lax.dot_general(left, right, (((0,), (0,)), ((), ())), preferred_element_...  42.2 us
    mul x1, other arithmetic, per_device(): lax.psum_scatter(gram_product(part, hidden), 'hb', scatter_dimension=0, t...  9.14 us
  transfers between devices with their start and end apart: 3, of which 2 were waited for; matrix products, arithmetic and copies ran while one was open for 11% of the time, Pallas kernels for 0%

commit v1 on v0

v1 whole, which is shorter than its diff:
```python
import functools

import jax
import jax.numpy as jnp
from jax import lax
from jax.experimental import pallas as pl
from jax.experimental.pallas import tpu as pltpu
from jax.sharding import PartitionSpec as P

MESH = pl.DeviceIdType.MESH
PIECES = 4


def gram_product(left, right):
    return lax.dot_general(
        left, right, (((0,), (0,)), ((), ())), preferred_element_type=jnp.float32
    )


def gather_kernel(n_tp, n_hb, normed, hidden, rows, units, cols,
                  local_sem, twin_send, peer_send, pass_send, rows_recv,
                  unit_send, unit_recv, line_send, line_recv, cross_send, cross_recv, own_sem):
    q = n_tp // n_hb
    n_y = n_hb // 2
    t, h = lax.axis_index("tp"), lax.axis_index("hb")
    z, x = t // q, t % q
    y, core = h // 2, h % 2
    twin = y * 2 + 1 - core
    tokens, width = normed.shape
    piece = tokens // PIECES
    n = n_hb * PIECES
    is_source = z == h
    goes_up = jnp.logical_and(z >= h, z < n_hb - 1)
    goes_down = jnp.logical_and(z <= h, z > 0)

    def other_y(d):
        return lax.rem(y + d, n_y) * 2 + core

    def from_y(d):
        return lax.rem(y - d + n_y, n_y) * 2 + core

    def at(group, s):
        return pl.ds(pl.multiple_of(group * tokens + s * piece, piece), piece)

    def block(ref, group):
        return ref.at[pl.ds(pl.multiple_of(group * tokens, tokens), tokens), :]

    def columns(position):
        return pl.ds(pl.multiple_of(position * width, width), width)

    def remote(src, dst, send, recv, where):
        return pltpu.make_async_remote_copy(
            src_ref=src, dst_ref=dst, send_sem=send, recv_sem=recv,
            device_id=where, device_id_type=MESH)

    barrier = pltpu.get_barrier_semaphore()

    def greet(where):
        pl.semaphore_signal(barrier, inc=1, device_id=where, device_id_type=MESH)

    greet({"hb": twin})
    for d in range(1, n_y):
        greet({"hb": other_y(d)})
    for d in range(1, q):
        greet({"tp": z * q + lax.rem(x + d, q)})
    pl.when(z > 0)(lambda: greet({"tp": t - q}))
    pl.when(z < n_hb - 1)(lambda: greet({"tp": t + q}))
    ends = jnp.where(z > 0, 1, 0) + jnp.where(z < n_hb - 1, 1, 0)
    pl.semaphore_wait(barrier, 1 + (n_y - 1) + (q - 1) + ends)

    own_rows = pltpu.make_async_copy(normed, block(rows, h), local_sem.at[0])
    own_units = pltpu.make_async_copy(hidden, block(units, h), local_sem.at[1])

    def own_piece(s):
        return normed.at[pl.ds(pl.multiple_of(s * piece, piece), piece), :]

    def to_twin(s):
        return remote(own_piece(s), rows.at[at(h, s), :], twin_send.at[s],
                      rows_recv.at[h * PIECES + s], {"hb": twin})

    def to_peer(d, s):
        return remote(own_piece(s), rows.at[at(h, s), :], peer_send.at[(d - 1) * PIECES + s],
                      rows_recv.at[h * PIECES + s], {"hb": other_y(d)})

    def pass_on(d, s):
        group = from_y(d)
        return remote(rows.at[at(group, s), :], rows.at[at(group, s), :],
                      pass_send.at[(d - 1) * PIECES + s],
                      rows_recv.at[group * PIECES + s], {"hb": twin})

    def rows_arrival(group, s):
        return remote(own_piece(s), rows.at[at(group, s), :], twin_send.at[s],
                      rows_recv.at[group * PIECES + s], {"hb": twin})

    def units_to(i, where):
        return remote(hidden, block(units, h), unit_send.at[i], unit_recv.at[h], {"hb": where})

    def units_pass(d):
        group = from_y(d)
        return remote(block(units, group), block(units, group), unit_send.at[n_y - 1 + d],
                      unit_recv.at[group], {"hb": twin})

    def units_arrival(group):
        return remote(hidden, block(units, group), unit_send.at[0], unit_recv.at[group],
                      {"hb": twin})

    def place(i):
        k, s = i // PIECES, i % PIECES
        hy, hc = k // 2, k % 2
        group = lax.rem(y + hy, n_y) * 2 + lax.rem(core + hc, 2)
        return group, s

    def line(i, src, step):
        group, s = place(i)
        return remote(src.at[at(group, s), columns(x) if src is cols else slice(None)],
                      cols.at[at(group, s), columns(x)],
                      line_send.at[(0 if step < 0 else n) + i], line_recv.at[i],
                      {"tp": t + step * q})

    def cross(i, src, d):
        group, s = place(i)
        return remote(src.at[at(group, s), columns(x) if src is cols else slice(None)],
                      cols.at[at(group, s), columns(x)],
                      cross_send.at[(d - 1) * n + i], cross_recv.at[(d - 1) * n + i],
                      {"tp": z * q + lax.rem(x + d, q)})

    def cross_arrival(i, d):
        group, s = place(i)
        there = cols.at[at(group, s), columns(lax.rem(x - d + q, q))]
        return remote(there, there, cross_send.at[(d - 1) * n + i],
                      cross_recv.at[(d - 1) * n + i], {"tp": z * q + lax.rem(x + d, q)})

    def own_columns(i):
        group, s = place(i)
        return pltpu.make_async_copy(rows.at[at(group, s), :], cols.at[at(group, s), columns(x)],
                                     own_sem.at[i])

    own_rows.start()
    for d in range(1, n_y):
        for s in range(PIECES):
            to_peer(d, s).start()
    for s in range(PIECES):
        to_twin(s).start()
    own_units.start()
    own_rows.wait()

    def hand_out(i, src):
        pl.when(goes_up)(lambda: line(i, src, 1).start())
        pl.when(goes_down)(lambda: line(i, src, -1).start())
        for d in range(1, q):
            cross(i, src, d).start()

    def step(i):
        group, s = place(i)

        @pl.when(is_source)
        def _():
            awaited = jnp.logical_and(i >= PIECES, (i // PIECES) % 2 == 1)
            pl.when(awaited)(lambda: rows_arrival(group, s).wait_recv())
            hand_out(i, rows)
            own_columns(i).start()

        @pl.when(jnp.logical_not(is_source))
        def _():
            line(i, cols, 1).wait_recv()
            hand_out(i, cols)

    n_first = (n_y - 1) * PIECES

    def first(i, carry):
        step(i)
        d, s = i // PIECES + 1, i % PIECES
        rows_arrival(from_y(d), s).wait_recv()
        pass_on(d, s).start()
        return carry

    def later(i, carry):
        step(i)
        return carry

    lax.fori_loop(0, n_first, first, 0)
    units_to(0, twin).start()
    for d in range(1, n_y):
        units_to(d, other_y(d)).start()
    n_second = max(n_first, n * 3 // 4)
    lax.fori_loop(n_first, n_second, later, 0)
    for d in range(1, n_y):
        units_arrival(from_y(d)).wait_recv()
        units_pass(d).start()
    lax.fori_loop(n_second, n, later, 0)

    def finish_rows(i, carry):
        group, s = place(i)
        pl.when(jnp.logical_and((i // PIECES) % 2 == 1, jnp.logical_not(is_source)))(
            lambda: rows_arrival(group, s).wait_recv())
        return carry

    lax.fori_loop(0, n, finish_rows, 0)
    for k in range(n_y):
        units_arrival(lax.rem(y + k, n_y) * 2 + 1 - core).wait_recv()

    def finish(i, carry):
        for d in range(1, q):
            cross_arrival(i, d).wait_recv()
            cross(i, cols, d).wait_send()
        pl.when(goes_up)(lambda: line(i, cols, 1).wait_send())
        pl.when(goes_down)(lambda: line(i, cols, -1).wait_send())
        pl.when(is_source)(lambda: own_columns(i).wait())
        return carry

    lax.fori_loop(0, n, finish, 0)
    own_units.wait()
    for s in range(PIECES):
        to_twin(s).wait_send()
        for d in range(1, n_y):
            to_peer(d, s).wait_send()
            pass_on(d, s).wait_send()
    units_to(0, twin).wait_send()
    for d in range(1, n_y):
        units_to(d, other_y(d)).wait_send()
        units_pass(d).wait_send()


def gather(normed, hidden):
    n_tp, n_hb = lax.axis_size("tp"), lax.axis_size("hb")
    q, n_y = n_tp // n_hb, n_hb // 2
    tokens, width = normed.shape
    n = n_hb * PIECES
    dma = pltpu.SemaphoreType.DMA
    anywhere = pl.BlockSpec(memory_space=pl.ANY)
    far = max(1, (n_y - 1) * PIECES)
    return pl.pallas_call(
        functools.partial(gather_kernel, n_tp, n_hb),
        out_shape=(
            jax.ShapeDtypeStruct((n_hb * tokens, width), normed.dtype),
            jax.ShapeDtypeStruct((n_hb * tokens, hidden.shape[1]), hidden.dtype),
            jax.ShapeDtypeStruct((n_hb * tokens, q * width), normed.dtype),
        ),
        in_specs=[anywhere] * 2,
        out_specs=(anywhere,) * 3,
        scratch_shapes=[
            dma((2,)), dma((PIECES,)), dma((far,)), dma((far,)), dma((n,)),
            dma((2 * n_y,)), dma((n_hb,)), dma((2 * n,)), dma((n,)),
            dma((max(1, q - 1) * n,)), dma((max(1, q - 1) * n,)), dma((n,)),
        ],
        compiler_params=pltpu.CompilerParams(collective_id=0, has_side_effects=True),
    )(normed, hidden)


def per_device(normed, hidden):
    groups = lax.axis_size("hb")
    scale = 2.0 / (normed.shape[0] * groups)
    rows, units, cols = gather(normed, hidden)
    h_in = gram_product(rows, cols) * scale
    own = hidden.shape[1] // groups
    mine = lax.dynamic_slice_in_dim(units, lax.axis_index("hb") * own, own, axis=1)
    h_down = gram_product(mine, units) * scale
    return (h_in, h_down)


def solution(mesh):
    return jax.shard_map(
        per_device,
        mesh=mesh,
        in_specs=(P("hb", "tp"), P("hb", "tp")),
        out_specs=(P("tp", "hb"), P(("tp", "hb"), None)),
        check_vma=False,
    )
```

time: 443 us -> 137 us (0.31)
  the two profiles are of different devices: /device:TPU:24 before, /device:TPU:0 now
where the time goes in v1:
time: 137 us
  Pallas kernels  111 us (81%)
  matrix products  25.3 us (18%)
    pallas_call x1, Pallas kernels, gather(): pl.pallas_call(functools.partial(gather_kernel, n_tp, n_hb), out_shape=(j...  111 us
    dot_general x2, matrix products, gram_product(): lax.dot_general(left, right, (((0,), (0,)), ((), ())), preferred_element_...  25.3 us

profile of v1, /device:TPU:0, one launch (start us, length us, event | category | flops | bytes accessed | tf_op | source)
XLA Modules:
  0.0 136.6 jit_solution(14214789141841186479)
XLA Ops:
  0.6 110.6 %shard_map.41 = (bf16[512,2048]{1,0:T(8,128)(2,1)}, bf16[512,3328]{1,0:T(8,128)(2,1)}, bf16[512,4096]{1,0:T(8,128)(2,1)}) custom-call(bf16[128,2048]{1,0:T(8,128)(2,1)} %normed.1, bf16[128,3328]{1,0:T(8,128)(2,1)} %hidden.1), custom_call_target="tpu_custom_call" | custom-call | tf_op jit(solution)/shard_map/pallas_call | solution.py:232
  111.3 0.0 copy-start
  111.3 18.9 %convolution_multiply_fusion = f32[2048,4096]{1,0:T(8,128)} fusion(bf16[512,2048]{1,0:T(8,128)(2,1)} %get-tuple-element.5, bf16[512,4096]{1,0:T(8,128)(2,1)} %get-tuple-element.6), kind=kOutput, calls=%fused_computation | convolution fusion | flops 8598323200 | bytes 39845888 | tf_op jit(solution)/shard_map/dot_general | solution.py:15
  130.2 0.0 copy-done
  130.2 6.3 %convolution_multiply_fusion.1 = f32[832,3328]{1,0:T(8,128)} fusion(bf16[512,3328]{1,0:T(8,128)(2,1)S(1)} %copy-done, s32[]{:T(128)S(6)} %select_n.3), kind=kOutput, calls=%fused_computation.1 | convolution fusion | flops 2838118400 | bytes 15400964 | tf_op jit(solution)/shard_map/dot_general | solution.py:15
Async XLA Ops:
  111.3 18.9 %copy-start = (bf16[512,3328]{1,0:T(8,128)(2,1)S(1)}, bf16[512,3328]{1,0:T(8,128)(2,1)}, u32[]{:S(2)}) copy-start(bf16[512,3328]{1,0:T(8,128)(2,1)} %get-tuple-element.7) | copy-start | bytes 10223620

commit v2 on v1

--- a/solution.py
+++ b/solution.py
@@ -9,12 +9,6 @@
 
 MESH = pl.DeviceIdType.MESH
 PIECES = 4
-
-
-def gram_product(left, right):
-    return lax.dot_general(
-        left, right, (((0,), (0,)), ((), ())), preferred_element_type=jnp.float32
-    )
 
 
 def gather_kernel(n_tp, n_hb, normed, hidden, rows, units, cols,
@@ -247,14 +241,92 @@
     )(normed, hidden)
 
 
+def tile_of(width):
+    return 256 if width % 256 == 0 else 128
+
+
+def window_of(own, width):
+    return min(width, -(-(own + 120) // 128) * 128)
+
+
+def product_kernel(n_down, scale, rows, units_tile, units, cols_tile, down, h_in,
+                   rows_in, rows_t, window, window_t, mine_t, sem):
+    i = pl.program_id(0)
+    width = units.shape[1]
+    own, span = mine_t.shape[0], window.shape[1]
+    first = lax.axis_index("hb") * own
+    start = jnp.minimum(first // 128 * 128, width - span)
+    get_window = pltpu.make_async_copy(
+        units.at[:, pl.ds(pl.multiple_of(start, 128), span)], window, sem.at[0])
+    get_rows = pltpu.make_async_copy(rows, rows_in, sem.at[1])
+
+    @pl.when(i == 0)
+    def _():
+        get_window.start()
+        get_rows.start()
+        get_window.wait()
+        window_t[...] = window[...].T.astype(jnp.float32)
+        mine_t[...] = window_t[pl.ds(pl.multiple_of(first - start, 8), own), :].astype(mine_t.dtype)
+
+    @pl.when(i < n_down)
+    def _():
+        down[...] = scale * jnp.dot(
+            mine_t[...], units_tile[...], preferred_element_type=jnp.float32)
+
+    @pl.when(i == n_down)
+    def _():
+        get_rows.wait()
+        rows_t[...] = rows_in[...].T
+
+    @pl.when(i >= n_down)
+    def _():
+        h_in[...] = scale * jnp.dot(
+            rows_t[...], cols_tile[...], preferred_element_type=jnp.float32)
+
+
+def products(rows, units, cols, scale):
+    n_hb = lax.axis_size("hb")
+    tokens, high = rows.shape
+    own = units.shape[1] // n_hb
+    down_tile, in_tile = tile_of(units.shape[1]), tile_of(cols.shape[1])
+    n_down, n_in = units.shape[1] // down_tile, cols.shape[1] // in_tile
+    span = window_of(own, units.shape[1])
+    anywhere = pl.BlockSpec(memory_space=pl.ANY)
+    early = lambda i: (0, jnp.minimum(i, n_down - 1))
+    late = lambda i: (0, jnp.maximum(i - n_down, 0))
+    return pl.pallas_call(
+        functools.partial(product_kernel, n_down, scale),
+        grid=(n_down + n_in,),
+        out_shape=(
+            jax.ShapeDtypeStruct((own, units.shape[1]), jnp.float32),
+            jax.ShapeDtypeStruct((high, cols.shape[1]), jnp.float32),
+        ),
+        in_specs=[
+            anywhere,
+            pl.BlockSpec((tokens, down_tile), early),
+            anywhere,
+            pl.BlockSpec((tokens, in_tile), late),
+        ],
+        out_specs=(
+            pl.BlockSpec((own, down_tile), early),
+            pl.BlockSpec((high, in_tile), late),
+        ),
+        scratch_shapes=[
+            pltpu.VMEM((tokens, high), rows.dtype),
+            pltpu.VMEM((high, tokens), rows.dtype),
+            pltpu.VMEM((tokens, span), units.dtype),
+            pltpu.VMEM((span, tokens), jnp.float32),
+            pltpu.VMEM((own, tokens), units.dtype),
+            pltpu.SemaphoreType.DMA((2,)),
+        ],
+        compiler_params=pltpu.CompilerParams(vmem_limit_bytes=40 * 2**20),
+    )(rows, units, units, cols)
+
+
 def per_device(normed, hidden):
-    groups = lax.axis_size("hb")
-    scale = 2.0 / (normed.shape[0] * groups)
+    scale = 2.0 / (normed.shape[0] * lax.axis_size("hb"))
     rows, units, cols = gather(normed, hidden)
-    h_in = gram_product(rows, cols) * scale
-    own = hidden.shape[1] // groups
-    mine = lax.dynamic_slice_in_dim(units, lax.axis_index("hb") * own, own, axis=1)
-    h_down = gram_product(mine, units) * scale
+    h_down, h_in = products(rows, units, cols, scale)
     return (h_in, h_down)
 
 

time: 137 us -> 145 us (1.058)
  Pallas kernels: 111 us -> 138 us
  matrix products: 25.3 us -> 0 us
  local copies, waits for them, and re-layouts: 0.01 us -> 5.73 us
    pallas_call x0 -> x1, Pallas kernels: none -> 27.6 us  [products(): pl.pallas_call(functools.partial(product_kernel, n_down, scale), grid=(n_...]
    dot_general x2 -> x0, matrix products: 25.3 us -> none  [gram_product(): lax.dot_general(left, right, (((0,), (0,)), ((), ())), preferred_element_...]
    unnamed x2 -> x6, local copies, waits for them, and re-layouts: 0.01 us -> 5.73 us
where the time goes in v2:
time: 145 us
  Pallas kernels  138 us (95%)
  local copies, waits for them, and re-layouts  5.73 us (4%)
    pallas_call x1, Pallas kernels, gather(): pl.pallas_call(functools.partial(gather_kernel, n_tp, n_hb), out_shape=(j...  111 us
    pallas_call x1, Pallas kernels, products(): pl.pallas_call(functools.partial(product_kernel, n_down, scale), grid=(n_...  27.6 us
    unnamed x6, local copies, waits for them, and re-layouts  5.73 us

profile of v2, /device:TPU:0, one launch (start us, length us, event | category | flops | bytes accessed | tf_op | source)
XLA Modules:
  0.0 144.6 jit_solution(12013588803738237452)
XLA Ops:
  0.6 110.6 %shard_map.41 = (bf16[512,2048]{1,0:T(8,128)(2,1)}, bf16[512,3328]{1,0:T(8,128)(2,1)}, bf16[512,4096]{1,0:T(8,128)(2,1)}) custom-call(bf16[128,2048]{1,0:T(8,128)(2,1)} %normed.1, bf16[128,3328]{1,0:T(8,128)(2,1)} %hidden.1), custom_call_target="tpu_custom_call" | custom-call | tf_op jit(solution)/shard_map/pallas_call | solution.py:226
  111.3 0.0 copy-start
  111.3 2.0 %copy-done = bf16[512,3328]{1,0:T(8,128)(2,1)S(1)} copy-done((bf16[512,3328]{1,0:T(8,128)(2,1)S(1)}, bf16[512,3328]{1,0:T(8,128)(2,1)}, u32[]{:S(2)}) %copy-start) | copy-done | bytes 3407896
  113.2 0.0 copy-start.1
  113.2 2.2 %copy-done.1 = bf16[512,4096]{1,0:T(8,128)(2,1)S(1)} copy-done((bf16[512,4096]{1,0:T(8,128)(2,1)S(1)}, bf16[512,4096]{1,0:T(8,128)(2,1)}, u32[]{:S(2)}) %copy-start.1) | copy-done | bytes 4194328
  115.4 0.0 copy-start.2
  115.4 1.6 %copy-done.2 = bf16[512,2048]{1,0:T(8,128)(2,1)S(1)} copy-done((bf16[512,2048]{1,0:T(8,128)(2,1)S(1)}, bf16[512,2048]{1,0:T(8,128)(2,1)}, u32[]{:S(2)}) %copy-start.2) | copy-done | bytes 2097176
  117.0 27.6 %shard_map.42 = (f32[832,3328]{1,0:T(8,128)}, f32[2048,4096]{1,0:T(8,128)}) custom-call(bf16[512,2048]{1,0:T(8,128)(2,1)S(1)} %copy-done.2, bf16[512,3328]{1,0:T(8,128)(2,1)S(1)} %copy-done, bf16[512,3328]{1,0:T(8,128)(2,1)S(1)} %copy-done, bf16[512,4096]{1,0:T(8,128)(2,1)S(1)} %copy-done.1), custom_call_target="tpu_custom_call" | custom-call | tf_op jit(solution)/shard_map/pallas_call | solution.py:297
Async XLA Ops:
  111.3 2.0 %copy-start = (bf16[512,3328]{1,0:T(8,128)(2,1)S(1)}, bf16[512,3328]{1,0:T(8,128)(2,1)}, u32[]{:S(2)}) copy-start(bf16[512,3328]{1,0:T(8,128)(2,1)} %get-tuple-element.8.units_tile.units) | copy-start | bytes 10223620
  113.2 2.2 %copy-start.1 = (bf16[512,4096]{1,0:T(8,128)(2,1)S(1)}, bf16[512,4096]{1,0:T(8,128)(2,1)}, u32[]{:S(2)}) copy-start(bf16[512,4096]{1,0:T(8,128)(2,1)} %get-tuple-element.9.cols_tile) | copy-start | bytes 12582916
  115.4 1.6 %copy-start.2 = (bf16[512,2048]{1,0:T(8,128)(2,1)S(1)}, bf16[512,2048]{1,0:T(8,128)(2,1)}, u32[]{:S(2)}) copy-start(bf16[512,2048]{1,0:T(8,128)(2,1)} %get-tuple-element.7.rows) | copy-start | bytes 6291460

commit v3 on v1

--- a/solution.py
+++ b/solution.py
@@ -11,15 +11,19 @@
 PIECES = 4
 
 
-def gram_product(left, right):
-    return lax.dot_general(
-        left, right, (((0,), (0,)), ((), ())), preferred_element_type=jnp.float32
-    )
-
-
-def gather_kernel(n_tp, n_hb, normed, hidden, rows, units, cols,
+def tile_of(width):
+    return 256 if width % 256 == 0 else 128
+
+
+def window_of(own, width):
+    return min(width, -(-(own + 120) // 128) * 128)
+
+
+def gather_kernel(n_tp, n_hb, scale, normed, hidden, rows_out, mine_out, units_out, cols_out,
+                  rows, units, cols, rows_t, window_t, mine_t,
                   local_sem, twin_send, peer_send, pass_send, rows_recv,
-                  unit_send, unit_recv, line_send, line_recv, cross_send, cross_recv, own_sem):
+                  unit_send, unit_recv, line_send, line_recv, cross_send, cross_recv,
+                  out_sem, cross_out_sem):
     q = n_tp // n_hb
     n_y = n_hb // 2
     t, h = lax.axis_index("tp"), lax.axis_index("hb")
@@ -130,10 +134,25 @@
         return remote(there, there, cross_send.at[(d - 1) * n + i],
                       cross_recv.at[(d - 1) * n + i], {"tp": z * q + lax.rem(x + d, q)})
 
-    def own_columns(i):
-        group, s = place(i)
-        return pltpu.make_async_copy(rows.at[at(group, s), :], cols.at[at(group, s), columns(x)],
-                                     own_sem.at[i])
+    def columns_out(i):
+        group, s = place(i)
+        there = at(group, s), columns(x)
+        return pltpu.make_async_copy(cols.at[there], cols_out.at[there], out_sem.at[i])
+
+    def own_columns_out(i):
+        group, s = place(i)
+        return pltpu.make_async_copy(rows.at[at(group, s), :],
+                                     cols_out.at[at(group, s), columns(x)], out_sem.at[i])
+
+    def cross_out(i, d):
+        group, s = place(i)
+        there = at(group, s), columns(lax.rem(x - d + q, q))
+        return pltpu.make_async_copy(cols.at[there], cols_out.at[there],
+                                     cross_out_sem.at[(d - 1) * n + i])
+
+    rows_done = pltpu.make_async_copy(rows_t, rows_out, local_sem.at[2])
+    mine_done = pltpu.make_async_copy(mine_t, mine_out, local_sem.at[3])
+    units_done = pltpu.make_async_copy(units, units_out, local_sem.at[4])
 
     own_rows.start()
     for d in range(1, n_y):
@@ -144,6 +163,10 @@
     own_units.start()
     own_rows.wait()
 
+    tile = tile_of(width)
+    n_turns = width // tile
+    factor = jnp.asarray(scale, rows_t.dtype)
+
     def hand_out(i, src):
         pl.when(goes_up)(lambda: line(i, src, 1).start())
         pl.when(goes_down)(lambda: line(i, src, -1).start())
@@ -155,15 +178,16 @@
 
         @pl.when(is_source)
         def _():
-            awaited = jnp.logical_and(i >= PIECES, (i // PIECES) % 2 == 1)
+            awaited = jnp.logical_and(i < n - n_turns, (i // PIECES) % 2 == 1)
             pl.when(awaited)(lambda: rows_arrival(group, s).wait_recv())
             hand_out(i, rows)
-            own_columns(i).start()
+            own_columns_out(i).start()
 
         @pl.when(jnp.logical_not(is_source))
         def _():
             line(i, cols, 1).wait_recv()
             hand_out(i, cols)
+            columns_out(i).start()
 
     n_first = (n_y - 1) * PIECES
 
@@ -182,34 +206,72 @@
     units_to(0, twin).start()
     for d in range(1, n_y):
         units_to(d, other_y(d)).start()
-    n_second = max(n_first, n * 3 // 4)
-    lax.fori_loop(n_first, n_second, later, 0)
+
+    def finish_rows(i, carry):
+        group, s = place(i)
+        pl.when(jnp.logical_and((i // PIECES) % 2 == 1,
+                                jnp.logical_or(jnp.logical_not(is_source), i >= n - n_turns)))(
+            lambda: rows_arrival(group, s).wait_recv())
+        return carry
+
+    def turn(b):
+        part = pl.ds(pl.multiple_of(b * tile, tile), tile)
+        rows_t[part, :] = (rows[:, part].T * factor).astype(rows_t.dtype)
+
+    def last(i, carry):
+        step(i)
+        turn(i - (n - n_turns))
+        return carry
+
+    lax.fori_loop(n_first, n - n_turns, later, 0)
+    lax.fori_loop(0, n, finish_rows, 0)
+    middle = n - max(1, n_turns // 2)
+    lax.fori_loop(n - n_turns, middle, last, 0)
     for d in range(1, n_y):
         units_arrival(from_y(d)).wait_recv()
         units_pass(d).start()
-    lax.fori_loop(n_second, n, later, 0)
-
-    def finish_rows(i, carry):
-        group, s = place(i)
-        pl.when(jnp.logical_and((i // PIECES) % 2 == 1, jnp.logical_not(is_source)))(
-            lambda: rows_arrival(group, s).wait_recv())
-        return carry
-
-    lax.fori_loop(0, n, finish_rows, 0)
+    lax.fori_loop(middle, n, last, 0)
+    rows_done.start()
+
     for k in range(n_y):
         units_arrival(lax.rem(y + k, n_y) * 2 + 1 - core).wait_recv()
+    own_units.wait()
+    units_done.start()
+    own, span = mine_t.shape[0], window_t.shape[0]
+    first_column = h * own
+    start = jnp.minimum(first_column // 128 * 128, units.shape[1] - span)
+
+    def turn_units(b, carry):
+        there = pl.ds(pl.multiple_of(start + b * 128, 128), 128)
+        window_t[pl.ds(pl.multiple_of(b * 128, 128), 128), :] = (
+            units[:, there].T.astype(jnp.float32) * scale)
+        return carry
+
+    lax.fori_loop(0, span // 128, turn_units, 0)
+    mine_t[...] = window_t[pl.ds(pl.multiple_of(first_column - start, 8), own), :].astype(
+        mine_t.dtype)
+    mine_done.start()
 
     def finish(i, carry):
         for d in range(1, q):
             cross_arrival(i, d).wait_recv()
+            cross_out(i, d).start()
+        return carry
+
+    def finish_sends(i, carry):
+        for d in range(1, q):
             cross(i, cols, d).wait_send()
+            cross_out(i, d).wait()
         pl.when(goes_up)(lambda: line(i, cols, 1).wait_send())
         pl.when(goes_down)(lambda: line(i, cols, -1).wait_send())
-        pl.when(is_source)(lambda: own_columns(i).wait())
+        columns_out(i).wait()
         return carry
 
     lax.fori_loop(0, n, finish, 0)
-    own_units.wait()
+    lax.fori_loop(0, n, finish_sends, 0)
+    rows_done.wait()
+    mine_done.wait()
+    units_done.wait()
     for s in range(PIECES):
         to_twin(s).wait_send()
         for d in range(1, n_y):
@@ -221,40 +283,95 @@
         units_pass(d).wait_send()
 
 
-def gather(normed, hidden):
+def gather(normed, hidden, scale):
     n_tp, n_hb = lax.axis_size("tp"), lax.axis_size("hb")
     q, n_y = n_tp // n_hb, n_hb // 2
     tokens, width = normed.shape
+    units = hidden.shape[1]
+    own = units // n_hb
+    total = n_hb * tokens
     n = n_hb * PIECES
     dma = pltpu.SemaphoreType.DMA
-    anywhere = pl.BlockSpec(memory_space=pl.ANY)
+    anywhere = pl.BlockSpec(memory_space=pltpu.HBM)
     far = max(1, (n_y - 1) * PIECES)
+    crossings = max(1, q - 1) * n
+    kind = normed.dtype
     return pl.pallas_call(
-        functools.partial(gather_kernel, n_tp, n_hb),
+        functools.partial(gather_kernel, n_tp, n_hb, scale),
         out_shape=(
-            jax.ShapeDtypeStruct((n_hb * tokens, width), normed.dtype),
-            jax.ShapeDtypeStruct((n_hb * tokens, hidden.shape[1]), hidden.dtype),
-            jax.ShapeDtypeStruct((n_hb * tokens, q * width), normed.dtype),
+            jax.ShapeDtypeStruct((width, total), kind),
+            jax.ShapeDtypeStruct((own, total), kind),
+            jax.ShapeDtypeStruct((total, units), kind),
+            jax.ShapeDtypeStruct((total, q * width), kind),
         ),
         in_specs=[anywhere] * 2,
-        out_specs=(anywhere,) * 3,
+        out_specs=(anywhere,) * 4,
         scratch_shapes=[
-            dma((2,)), dma((PIECES,)), dma((far,)), dma((far,)), dma((n,)),
+            pltpu.VMEM((total, width), kind),
+            pltpu.VMEM((total, units), kind),
+            pltpu.VMEM((total, q * width), kind),
+            pltpu.VMEM((width, total), kind),
+            pltpu.VMEM((window_of(own, units), total), jnp.float32),
+            pltpu.VMEM((own, total), kind),
+            dma((5,)), dma((PIECES,)), dma((far,)), dma((far,)), dma((n,)),
             dma((2 * n_y,)), dma((n_hb,)), dma((2 * n,)), dma((n,)),
-            dma((max(1, q - 1) * n,)), dma((max(1, q - 1) * n,)), dma((n,)),
+            dma((crossings,)), dma((crossings,)), dma((n,)), dma((crossings,)),
         ],
-        compiler_params=pltpu.CompilerParams(collective_id=0, has_side_effects=True),
+        compiler_params=pltpu.CompilerParams(
+            collective_id=0, has_side_effects=True, vmem_limit_bytes=60 * 2**20),
     )(normed, hidden)
 
 
+def product_kernel(n_down, mine_t, units_tile, rows_t, cols_tile, down, h_in, rows_in, sem):
+    i = pl.program_id(0)
+    get_rows = pltpu.make_async_copy(rows_t, rows_in, sem)
+    pl.when(i == 0)(get_rows.start)
+
+    @pl.when(i < n_down)
+    def _():
+        down[...] = jnp.dot(mine_t[...], units_tile[...], preferred_element_type=jnp.float32)
+
+    pl.when(i == n_down)(get_rows.wait)
+
+    @pl.when(i >= n_down)
+    def _():
+        h_in[...] = jnp.dot(rows_in[...], cols_tile[...], preferred_element_type=jnp.float32)
+
+
+def products(rows_t, mine_t, units, cols):
+    own, tokens = mine_t.shape
+    high = rows_t.shape[0]
+    down_tile, in_tile = tile_of(units.shape[1]), tile_of(cols.shape[1])
+    n_down, n_in = units.shape[1] // down_tile, cols.shape[1] // in_tile
+    early = lambda i: (0, jnp.minimum(i, n_down - 1))
+    late = lambda i: (0, jnp.maximum(i - n_down, 0))
+    return pl.pallas_call(
+        functools.partial(product_kernel, n_down),
+        grid=(n_down + n_in,),
+        out_shape=(
+            jax.ShapeDtypeStruct((own, units.shape[1]), jnp.float32),
+            jax.ShapeDtypeStruct((high, cols.shape[1]), jnp.float32),
+        ),
+        in_specs=[
+            pl.BlockSpec((own, tokens), lambda i: (0, 0)),
+            pl.BlockSpec((tokens, down_tile), early),
+            pl.BlockSpec(memory_space=pltpu.HBM),
+            pl.BlockSpec((tokens, in_tile), late),
+        ],
+        out_specs=(
+            pl.BlockSpec((own, down_tile), early),
+            pl.BlockSpec((high, in_tile), late),
+        ),
+        scratch_shapes=[pltpu.VMEM((high, tokens), rows_t.dtype), pltpu.SemaphoreType.DMA],
+        compiler_params=pltpu.CompilerParams(vmem_limit_bytes=60 * 2**20),
+    )(mine_t, units, rows_t, cols)
+
+
 def per_device(normed, hidden):
-    groups = lax.axis_size("hb")
-    scale = 2.0 / (normed.shape[0] * groups)
-    rows, units, cols = gather(normed, hidden)
-    h_in = gram_product(rows, cols) * scale
-    own = hidden.shape[1] // groups
-    mine = lax.dynamic_slice_in_dim(units, lax.axis_index("hb") * own, own, axis=1)
-    h_down = gram_product(mine, units) * scale
+    total = normed.shape[0] * lax.axis_size("hb")
+    assert total & (total - 1) == 0
+    rows_t, mine_t, units, cols = gather(normed, hidden, 2.0 / total)
+    h_down, h_in = products(rows_t, mine_t, units, cols)
     return (h_in, h_down)
 
 

time: 137 us -> 96 us (0.70)
  the two profiles are of different devices: /device:TPU:0 before, /device:TPU:24 now
where the time goes in v3:
time: 96 us; the launch traced here: 94.2 us
  Pallas kernels  93.6 us (98%)
    pallas_call x1, Pallas kernels, gather(): pl.pallas_call(functools.partial(gather_kernel, n_tp, n_hb, scale), out_s...  63.4 us
    pallas_call x1, Pallas kernels, products(): pl.pallas_call(functools.partial(product_kernel, n_down), grid=(n_down +...  30.2 us

profile of v3, /device:TPU:24, one launch (start us, length us, event | category | flops | bytes accessed | tf_op | source)
XLA Modules:
  0.0 94.2 jit_solution(3245322339819819721)
XLA Ops:
  0.6 63.4 %shard_map.41 = (bf16[2048,512]{1,0:T(8,128)(2,1)}, bf16[832,512]{1,0:T(8,128)(2,1)}, bf16[512,3328]{1,0:T(8,128)(2,1)}, bf16[512,4096]{1,0:T(8,128)(2,1)}) custom-call(bf16[128,2048]{1,0:T(8,128)(2,1)} %normed.1, bf16[128,3328]{1,0:T(8,128)(2,1)} %hidden.1), custom_call_target="tpu_custom_call" | custom-call | tf_op jit(solution)/shard_map/pallas_call | solution.py:299
  64.0 30.2 %shard_map.42 = (f32[832,3328]{1,0:T(8,128)}, f32[2048,4096]{1,0:T(8,128)}) custom-call(bf16[832,512]{1,0:T(8,128)(2,1)} %get-tuple-element.8.mine_t, bf16[512,3328]{1,0:T(8,128)(2,1)} %get-tuple-element.9.units_tile, bf16[2048,512]{1,0:T(8,128)(2,1)} %get-tuple-element.10.rows_t, bf16[512,4096]{1,0:T(8,128)(2,1)} %get-tuple-element.11.cols_tile), custom_call_target="tpu_custom_call" | custom-call | tf_op jit(solution)/shard_map/pallas_call | solution.py:348

commit v4 on v3

--- a/solution.py
+++ b/solution.py
@@ -322,47 +322,87 @@
     )(normed, hidden)
 
 
-def product_kernel(n_down, mine_t, units_tile, rows_t, cols_tile, down, h_in, rows_in, sem):
-    i = pl.program_id(0)
-    get_rows = pltpu.make_async_copy(rows_t, rows_in, sem)
-    pl.when(i == 0)(get_rows.start)
-
-    @pl.when(i < n_down)
-    def _():
-        down[...] = jnp.dot(mine_t[...], units_tile[...], preferred_element_type=jnp.float32)
-
-    pl.when(i == n_down)(get_rows.wait)
-
-    @pl.when(i >= n_down)
-    def _():
-        h_in[...] = jnp.dot(rows_in[...], cols_tile[...], preferred_element_type=jnp.float32)
+def part_of(size, unit, most):
+    sizes = [p for p in range(unit, most + 1, unit) if size % p == 0]
+    return sizes[-1] if sizes else size
+
+
+def product_kernel(slots, mine_t, units, rows_t, cols, down, h_in,
+                   mine_v, units_v, rows_v, cols_v, down_v, h_in_v,
+                   left_sem, units_sem, cols_sem, down_sem, h_in_sem):
+    get_mine = pltpu.make_async_copy(mine_t, mine_v, left_sem.at[0])
+    get_rows = pltpu.make_async_copy(rows_t, rows_v, left_sem.at[1])
+
+    def get(src, dst, sems, j, wide):
+        there = pl.ds(pl.multiple_of(j * wide, 128), wide)
+        return pltpu.make_async_copy(src.at[:, there], dst.at[:, there], sems.at[j])
+
+    def product(left, right, right_hbm, right_sems, out, out_v, out_sems):
+        high, wide = out_v.shape[1:]
+        n_high, n_wide = out.shape[0] // high, out.shape[1] // wide
+        n = n_high * n_wide
+
+        def put(i):
+            slot = i % slots
+            down_by = pl.ds(pl.multiple_of((i % n_high) * high, 8), high)
+            along = pl.ds(pl.multiple_of((i // n_high) * wide, 128), wide)
+            return pltpu.make_async_copy(out_v.at[slot], out.at[down_by, along], out_sems.at[slot])
+
+        def step(i, carry):
+            m, j = i % n_high, i // n_high
+            pl.when(m == 0)(lambda: get(right_hbm, right, right_sems, j, wide).wait())
+            pl.when(i >= slots)(lambda: put(i - slots).wait())
+            rows_here = left[pl.ds(pl.multiple_of(m * high, 8), high), :]
+            columns_here = right[:, pl.ds(pl.multiple_of(j * wide, 128), wide)]
+            out_v[i % slots] = jnp.dot(
+                rows_here, columns_here, preferred_element_type=jnp.float32)
+            put(i).start()
+            return carry
+
+        lax.fori_loop(0, n, step, 0)
+        return [put(i) for i in range(max(0, n - slots), n)]
+
+    units_wide, cols_wide = down_v.shape[2], h_in_v.shape[2]
+    get_mine.start()
+    for j in range(units.shape[1] // units_wide):
+        get(units, units_v, units_sem, j, units_wide).start()
+    get_rows.start()
+    for j in range(cols.shape[1] // cols_wide):
+        get(cols, cols_v, cols_sem, j, cols_wide).start()
+    get_mine.wait()
+    puts = product(mine_v, units_v, units, units_sem, down, down_v, down_sem)
+    get_rows.wait()
+    puts += product(rows_v, cols_v, cols, cols_sem, h_in, h_in_v, h_in_sem)
+    for put in puts:
+        put.wait()
 
 
 def products(rows_t, mine_t, units, cols):
     own, tokens = mine_t.shape
     high = rows_t.shape[0]
-    down_tile, in_tile = tile_of(units.shape[1]), tile_of(cols.shape[1])
-    n_down, n_in = units.shape[1] // down_tile, cols.shape[1] // in_tile
-    early = lambda i: (0, jnp.minimum(i, n_down - 1))
-    late = lambda i: (0, jnp.maximum(i - n_down, 0))
+    slots = 4
+    down_tile = part_of(own, 16, 512), part_of(units.shape[1], 128, 1664)
+    in_tile = part_of(high, 16, 512), part_of(cols.shape[1], 128, 1024)
+    in_hbm = pl.BlockSpec(memory_space=pltpu.HBM)
+    dma = pltpu.SemaphoreType.DMA
     return pl.pallas_call(
-        functools.partial(product_kernel, n_down),
-        grid=(n_down + n_in,),
+        functools.partial(product_kernel, slots),
         out_shape=(
             jax.ShapeDtypeStruct((own, units.shape[1]), jnp.float32),
             jax.ShapeDtypeStruct((high, cols.shape[1]), jnp.float32),
         ),
-        in_specs=[
-            pl.BlockSpec((own, tokens), lambda i: (0, 0)),
-            pl.BlockSpec((tokens, down_tile), early),
-            pl.BlockSpec(memory_space=pltpu.HBM),
-            pl.BlockSpec((tokens, in_tile), late),
+        in_specs=[in_hbm] * 4,
+        out_specs=(in_hbm,) * 2,
+        scratch_shapes=[
+            pltpu.VMEM(mine_t.shape, mine_t.dtype),
+            pltpu.VMEM(units.shape, units.dtype),
+            pltpu.VMEM(rows_t.shape, rows_t.dtype),
+            pltpu.VMEM(cols.shape, cols.dtype),
+            pltpu.VMEM((slots, *down_tile), jnp.float32),
+            pltpu.VMEM((slots, *in_tile), jnp.float32),
+            dma((2,)), dma((units.shape[1] // down_tile[1],)),
+            dma((cols.shape[1] // in_tile[1],)), dma((slots,)), dma((slots,)),
         ],
-        out_specs=(
-            pl.BlockSpec((own, down_tile), early),
-            pl.BlockSpec((high, in_tile), late),
-        ),
-        scratch_shapes=[pltpu.VMEM((high, tokens), rows_t.dtype), pltpu.SemaphoreType.DMA],
         compiler_params=pltpu.CompilerParams(vmem_limit_bytes=60 * 2**20),
     )(mine_t, units, rows_t, cols)
 

time: 96 us -> 84.3 us (0.88)
  Pallas kernels: 93.6 us -> 82.5 us
    pallas_call x1, Pallas kernels: 30.2 us -> 19.1 us  [products(): pl.pallas_call(functools.partial(product_kernel, slots), out_shape=(jax.S...]
where the time goes in v4:
time: 84.3 us; the launch traced here: 83.2 us
  Pallas kernels  82.5 us (98%)
    pallas_call x1, Pallas kernels, gather(): pl.pallas_call(functools.partial(gather_kernel, n_tp, n_hb, scale), out_s...  63.4 us
    pallas_call x1, Pallas kernels, products(): pl.pallas_call(functools.partial(product_kernel, slots), out_shape=(jax.S...  19.1 us

profile of v4, /device:TPU:24, one launch (start us, length us, event | category | flops | bytes accessed | tf_op | source)
XLA Modules:
  0.0 83.2 jit_solution(13676038403298836839)
XLA Ops:
  0.6 63.4 %shard_map.41 = (bf16[2048,512]{1,0:T(8,128)(2,1)}, bf16[832,512]{1,0:T(8,128)(2,1)}, bf16[512,3328]{1,0:T(8,128)(2,1)}, bf16[512,4096]{1,0:T(8,128)(2,1)}) custom-call(bf16[128,2048]{1,0:T(8,128)(2,1)} %normed.1, bf16[128,3328]{1,0:T(8,128)(2,1)} %hidden.1), custom_call_target="tpu_custom_call" | custom-call | tf_op jit(solution)/shard_map/pallas_call | solution.py:299
  64.0 19.1 %shard_map.42 = (f32[832,3328]{1,0:T(8,128)}, f32[2048,4096]{1,0:T(8,128)}) custom-call(bf16[832,512]{1,0:T(8,128)(2,1)} %get-tuple-element.8.mine_t, bf16[512,3328]{1,0:T(8,128)(2,1)} %get-tuple-element.9.units, bf16[2048,512]{1,0:T(8,128)(2,1)} %get-tuple-element.10.rows_t, bf16[512,4096]{1,0:T(8,128)(2,1)} %get-tuple-element.11.cols), custom_call_target="tpu_custom_call" | custom-call | tf_op jit(solution)/shard_map/pallas_call | solution.py:388

commit v5 on v4

--- a/solution.py
+++ b/solution.py
@@ -20,10 +20,10 @@
 
 
 def gather_kernel(n_tp, n_hb, scale, normed, hidden, rows_out, mine_out, units_out, cols_out,
-                  rows, units, cols, rows_t, window_t, mine_t,
+                  rows, units, cols, rows_t, window_t, mine_t, relayed,
                   local_sem, twin_send, peer_send, pass_send, rows_recv,
                   unit_send, unit_recv, line_send, line_recv, cross_send, cross_recv,
-                  out_sem, cross_out_sem):
+                  out_sem, cross_out_sem, relay_send, relay_recv, over_send):
     q = n_tp // n_hb
     n_y = n_hb // 2
     t, h = lax.axis_index("tp"), lax.axis_index("hb")
@@ -37,11 +37,30 @@
     goes_up = jnp.logical_and(z >= h, z < n_hb - 1)
     goes_down = jnp.logical_and(z <= h, z > 0)
 
+    half = n // 2
+    relief = n_hb == 4
+    is_up, is_down = h == 3, h == 0
+    relay_source = jnp.logical_or(jnp.logical_and(is_up, z == 1), jnp.logical_and(is_down, z == 2))
+    relay_middle = jnp.logical_or(jnp.logical_and(is_up, z == 2), jnp.logical_and(is_down, z == 1))
+    relay_end = jnp.logical_or(jnp.logical_and(is_up, z == 3), jnp.logical_and(is_down, z == 0))
+    relay_sends = jnp.logical_or(relay_source, relay_middle)
+    relay_receives = jnp.logical_or(relay_middle, relay_end)
+
+    def sends_up(i):
+        if not relief:
+            return goes_up
+        return jnp.logical_and(goes_up, jnp.logical_or(h != 1, i < half))
+
+    def sends_down(i):
+        if not relief:
+            return goes_down
+        return jnp.logical_and(goes_down, jnp.logical_or(h != 2, i < half))
+
     def other_y(d):
         return lax.rem(y + d, n_y) * 2 + core
 
     def from_y(d):
-        return lax.rem(y - d + n_y, n_y) * 2 + core
+        return other_y(d)
 
     def at(group, s):
         return pl.ds(pl.multiple_of(group * tokens + s * piece, piece), piece)
@@ -168,10 +187,38 @@
     factor = jnp.asarray(scale, rows_t.dtype)
 
     def hand_out(i, src):
-        pl.when(goes_up)(lambda: line(i, src, 1).start())
-        pl.when(goes_down)(lambda: line(i, src, -1).start())
+        pl.when(sends_up(i))(lambda: line(i, src, 1).start())
+        pl.when(sends_down(i))(lambda: line(i, src, -1).start())
         for d in range(1, q):
             cross(i, src, d).start()
+
+    def relay_piece(r):
+        return relayed.at[pl.ds(pl.multiple_of(r * piece, piece), piece), :]
+
+    def relay(r, src):
+        return remote(src, relay_piece(r), relay_send.at[r], relay_recv.at[r],
+                      {"tp": t + jnp.where(is_up, q, -q)})
+
+    def over(r):
+        group = y * 2 + lax.rem(core + r // PIECES, 2)
+        return remote(relay_piece(r), cols.at[at(group, r % PIECES), columns(x)],
+                      over_send.at[r], line_recv.at[half + r], {"hb": other_y(1)})
+
+    def relay_step(r):
+        @pl.when(relay_receives)
+        def _():
+            relay(r, relay_piece(r)).wait_recv()
+            pl.when(relay_middle)(lambda: relay(r, relay_piece(r)).start())
+            over(r).start()
+
+    if relief:
+        @pl.when(relay_source)
+        def _():
+            for s in range(PIECES):
+                relay(s, own_piece(s)).start()
+            for s in range(PIECES):
+                rows_arrival(twin, s).wait_recv()
+                relay(PIECES + s, rows.at[at(twin, s), :]).start()
 
     def step(i):
         group, s = place(i)
@@ -193,25 +240,34 @@
 
     def first(i, carry):
         step(i)
-        d, s = i // PIECES + 1, i % PIECES
+        d, s = i // PIECES, i % PIECES
         rows_arrival(from_y(d), s).wait_recv()
         pass_on(d, s).start()
+        if relief:
+            relay_step(i - PIECES)
         return carry
 
     def later(i, carry):
         step(i)
-        return carry
-
-    lax.fori_loop(0, n_first, first, 0)
+        if relief:
+            pl.when(jnp.logical_and(i >= PIECES, i < PIECES + half))(
+                lambda: relay_step(i - PIECES))
+        return carry
+
+    lax.fori_loop(0, PIECES, later, 0)
+    lax.fori_loop(PIECES, PIECES + n_first, first, 0)
     units_to(0, twin).start()
     for d in range(1, n_y):
         units_to(d, other_y(d)).start()
 
     def finish_rows(i, carry):
         group, s = place(i)
-        pl.when(jnp.logical_and((i // PIECES) % 2 == 1,
-                                jnp.logical_or(jnp.logical_not(is_source), i >= n - n_turns)))(
-            lambda: rows_arrival(group, s).wait_recv())
+        awaited = jnp.logical_and((i // PIECES) % 2 == 1,
+                                  jnp.logical_or(jnp.logical_not(is_source), i >= n - n_turns))
+        if relief:
+            awaited = jnp.logical_and(awaited, jnp.logical_or(jnp.logical_not(relay_source),
+                                                              i >= half))
+        pl.when(awaited)(lambda: rows_arrival(group, s).wait_recv())
         return carry
 
     def turn(b):
@@ -220,10 +276,12 @@
 
     def last(i, carry):
         step(i)
+        if relief:
+            pl.when(i < PIECES + half)(lambda: relay_step(i - PIECES))
         turn(i - (n - n_turns))
         return carry
 
-    lax.fori_loop(n_first, n - n_turns, later, 0)
+    lax.fori_loop(PIECES + n_first, n - n_turns, later, 0)
     lax.fori_loop(0, n, finish_rows, 0)
     middle = n - max(1, n_turns // 2)
     lax.fori_loop(n - n_turns, middle, last, 0)
@@ -262,13 +320,21 @@
         for d in range(1, q):
             cross(i, cols, d).wait_send()
             cross_out(i, d).wait()
-        pl.when(goes_up)(lambda: line(i, cols, 1).wait_send())
-        pl.when(goes_down)(lambda: line(i, cols, -1).wait_send())
+        pl.when(sends_up(i))(lambda: line(i, cols, 1).wait_send())
+        pl.when(sends_down(i))(lambda: line(i, cols, -1).wait_send())
         columns_out(i).wait()
         return carry
 
     lax.fori_loop(0, n, finish, 0)
     lax.fori_loop(0, n, finish_sends, 0)
+
+    def finish_relay(r, carry):
+        pl.when(relay_sends)(lambda: relay(r, relay_piece(r)).wait_send())
+        pl.when(relay_receives)(lambda: over(r).wait_send())
+        return carry
+
+    if relief:
+        lax.fori_loop(0, half, finish_relay, 0)
     rows_done.wait()
     mine_done.wait()
     units_done.wait()
@@ -313,9 +379,11 @@
             pltpu.VMEM((width, total), kind),
             pltpu.VMEM((window_of(own, units), total), jnp.float32),
             pltpu.VMEM((own, total), kind),
+            pltpu.VMEM((total // 2, width), kind),
             dma((5,)), dma((PIECES,)), dma((far,)), dma((far,)), dma((n,)),
             dma((2 * n_y,)), dma((n_hb,)), dma((2 * n,)), dma((n,)),
             dma((crossings,)), dma((crossings,)), dma((n,)), dma((crossings,)),
+            dma((n // 2,)), dma((n // 2,)), dma((n // 2,)),
         ],
         compiler_params=pltpu.CompilerParams(
             collective_id=0, has_side_effects=True, vmem_limit_bytes=60 * 2**20),

time: 84.3 us -> 115 us (1.36)
  Pallas kernels: 82.5 us -> 114 us
    pallas_call x1, Pallas kernels: 63.4 us -> 95.1 us  [gather(): pl.pallas_call(functools.partial(gather_kernel, n_tp, n_hb, scale), out_s...]
where the time goes in v5:
time: 115 us
  Pallas kernels  114 us (99%)
    pallas_call x1, Pallas kernels, gather(): pl.pallas_call(functools.partial(gather_kernel, n_tp, n_hb, scale), out_s...  95.1 us
    pallas_call x1, Pallas kernels, products(): pl.pallas_call(functools.partial(product_kernel, slots), out_shape=(jax.S...  19.1 us

profile of v5, /device:TPU:24, one launch (start us, length us, event | category | flops | bytes accessed | tf_op | source)
XLA Modules:
  0.0 114.8 jit_solution(15818169661181249868)
XLA Ops:
  0.6 95.1 %shard_map.41 = (bf16[2048,512]{1,0:T(8,128)(2,1)}, bf16[832,512]{1,0:T(8,128)(2,1)}, bf16[512,3328]{1,0:T(8,128)(2,1)}, bf16[512,4096]{1,0:T(8,128)(2,1)}) custom-call(bf16[128,2048]{1,0:T(8,128)(2,1)} %normed.1, bf16[128,3328]{1,0:T(8,128)(2,1)} %hidden.1), custom_call_target="tpu_custom_call" | custom-call | tf_op jit(solution)/shard_map/pallas_call | solution.py:365
  95.7 19.1 %shard_map.42 = (f32[832,3328]{1,0:T(8,128)}, f32[2048,4096]{1,0:T(8,128)}) custom-call(bf16[832,512]{1,0:T(8,128)(2,1)} %get-tuple-element.8.mine_t, bf16[512,3328]{1,0:T(8,128)(2,1)} %get-tuple-element.9.units, bf16[2048,512]{1,0:T(8,128)(2,1)} %get-tuple-element.10.rows_t, bf16[512,4096]{1,0:T(8,128)(2,1)} %get-tuple-element.11.cols), custom_call_target="tpu_custom_call" | custom-call | tf_op jit(solution)/shard_map/pallas_call | solution.py:456

commit v6 on v5

--- a/solution.py
+++ b/solution.py
@@ -49,12 +49,12 @@
     def sends_up(i):
         if not relief:
             return goes_up
-        return jnp.logical_and(goes_up, jnp.logical_or(h != 1, i < half))
+        return jnp.logical_and(goes_up, jnp.logical_or(h != 1, i // PIECES != 2))
 
     def sends_down(i):
         if not relief:
             return goes_down
-        return jnp.logical_and(goes_down, jnp.logical_or(h != 2, i < half))
+        return jnp.logical_and(goes_down, jnp.logical_or(h != 2, i // PIECES != 2))
 
     def other_y(d):
         return lax.rem(y + d, n_y) * 2 + core
@@ -200,8 +200,7 @@
                       {"tp": t + jnp.where(is_up, q, -q)})
 
     def over(r):
-        group = y * 2 + lax.rem(core + r // PIECES, 2)
-        return remote(relay_piece(r), cols.at[at(group, r % PIECES), columns(x)],
+        return remote(relay_piece(r), cols.at[at(h, r), columns(x)],
                       over_send.at[r], line_recv.at[half + r], {"hb": other_y(1)})
 
     def relay_step(r):
@@ -216,9 +215,6 @@
         def _():
             for s in range(PIECES):
                 relay(s, own_piece(s)).start()
-            for s in range(PIECES):
-                rows_arrival(twin, s).wait_recv()
-                relay(PIECES + s, rows.at[at(twin, s), :]).start()
 
     def step(i):
         group, s = place(i)
@@ -249,24 +245,18 @@
 
     def later(i, carry):
         step(i)
-        if relief:
-            pl.when(jnp.logical_and(i >= PIECES, i < PIECES + half))(
-                lambda: relay_step(i - PIECES))
         return carry
 
     lax.fori_loop(0, PIECES, later, 0)
-    lax.fori_loop(PIECES, PIECES + n_first, first, 0)
-    units_to(0, twin).start()
     for d in range(1, n_y):
         units_to(d, other_y(d)).start()
+    units_to(0, twin).start()
+    lax.fori_loop(PIECES, PIECES + n_first, first, 0)
 
     def finish_rows(i, carry):
         group, s = place(i)
         awaited = jnp.logical_and((i // PIECES) % 2 == 1,
                                   jnp.logical_or(jnp.logical_not(is_source), i >= n - n_turns))
-        if relief:
-            awaited = jnp.logical_and(awaited, jnp.logical_or(jnp.logical_not(relay_source),
-                                                              i >= half))
         pl.when(awaited)(lambda: rows_arrival(group, s).wait_recv())
         return carry
 
@@ -276,19 +266,15 @@
 
     def last(i, carry):
         step(i)
-        if relief:
-            pl.when(i < PIECES + half)(lambda: relay_step(i - PIECES))
         turn(i - (n - n_turns))
         return carry
 
     lax.fori_loop(PIECES + n_first, n - n_turns, later, 0)
     lax.fori_loop(0, n, finish_rows, 0)
-    middle = n - max(1, n_turns // 2)
-    lax.fori_loop(n - n_turns, middle, last, 0)
+    lax.fori_loop(n - n_turns, n, last, 0)
     for d in range(1, n_y):
         units_arrival(from_y(d)).wait_recv()
         units_pass(d).start()
-    lax.fori_loop(middle, n, last, 0)
     rows_done.start()
 
     for k in range(n_y):
@@ -334,7 +320,7 @@
         return carry
 
     if relief:
-        lax.fori_loop(0, half, finish_relay, 0)
+        lax.fori_loop(0, PIECES, finish_relay, 0)
     rows_done.wait()
     mine_done.wait()
     units_done.wait()
@@ -379,11 +365,11 @@
             pltpu.VMEM((width, total), kind),
             pltpu.VMEM((window_of(own, units), total), jnp.float32),
             pltpu.VMEM((own, total), kind),
-            pltpu.VMEM((total // 2, width), kind),
+            pltpu.VMEM((tokens, width), kind),
             dma((5,)), dma((PIECES,)), dma((far,)), dma((far,)), dma((n,)),
             dma((2 * n_y,)), dma((n_hb,)), dma((2 * n,)), dma((n,)),
             dma((crossings,)), dma((crossings,)), dma((n,)), dma((crossings,)),
-            dma((n // 2,)), dma((n // 2,)), dma((n // 2,)),
+            dma((PIECES,)), dma((PIECES,)), dma((PIECES,)),
         ],
         compiler_params=pltpu.CompilerParams(
             collective_id=0, has_side_effects=True, vmem_limit_bytes=60 * 2**20),

time: 115 us -> 92.3 us (0.80)
  Pallas kernels: 114 us -> 91.5 us
    pallas_call x1, Pallas kernels: 95.1 us -> 72.4 us  [gather(): pl.pallas_call(functools.partial(gather_kernel, n_tp, n_hb, scale), out_s...]
where the time goes in v6:
time: 92.3 us; the launch traced here: 92.2 us
  Pallas kernels  91.5 us (99%)
    pallas_call x1, Pallas kernels, gather(): pl.pallas_call(functools.partial(gather_kernel, n_tp, n_hb, scale), out_s...  72.4 us
    pallas_call x1, Pallas kernels, products(): pl.pallas_call(functools.partial(product_kernel, slots), out_shape=(jax.S...  19.1 us

profile of v6, /device:TPU:24, one launch (start us, length us, event | category | flops | bytes accessed | tf_op | source)
XLA Modules:
  0.0 92.2 jit_solution(11713248525637816178)
XLA Ops:
  0.6 72.4 %shard_map.41 = (bf16[2048,512]{1,0:T(8,128)(2,1)}, bf16[832,512]{1,0:T(8,128)(2,1)}, bf16[512,3328]{1,0:T(8,128)(2,1)}, bf16[512,4096]{1,0:T(8,128)(2,1)}) custom-call(bf16[128,2048]{1,0:T(8,128)(2,1)} %normed.1, bf16[128,3328]{1,0:T(8,128)(2,1)} %hidden.1), custom_call_target="tpu_custom_call" | custom-call | tf_op jit(solution)/shard_map/pallas_call | solution.py:351
  73.0 19.1 %shard_map.42 = (f32[832,3328]{1,0:T(8,128)}, f32[2048,4096]{1,0:T(8,128)}) custom-call(bf16[832,512]{1,0:T(8,128)(2,1)} %get-tuple-element.8.mine_t, bf16[512,3328]{1,0:T(8,128)(2,1)} %get-tuple-element.9.units, bf16[2048,512]{1,0:T(8,128)(2,1)} %get-tuple-element.10.rows_t, bf16[512,4096]{1,0:T(8,128)(2,1)} %get-tuple-element.11.cols), custom_call_target="tpu_custom_call" | custom-call | tf_op jit(solution)/shard_map/pallas_call | solution.py:442
